TPU v7x, 32 devices: a whole 2x2x4 slice. The times are simulated.
32 devices in a mesh: gx: 8 (over z, x), gy: 2 (over core), gz: 2 (over y).
Axes of the slice: x: 2, y: 2, z: 4, core: 2. Of those that a mesh axis runs over, the one named last changes fastest.
Arguments:
- tokens: bfloat16 [64, 32, 32, 192], P('gx', 'gy', 'gz'), may hold values from -6 to 6
- upstream: bfloat16 [64, 32, 32, 192], P('gx', 'gy', 'gz'), may hold values from -6 to 6
- norm_gain: float32 [192], replicated, may hold values from 0.25 to 1.75
- norm_bias: float32 [192], replicated, may hold values from -3 to 3
- qkv_weight: bfloat16 [192, 576], replicated, may hold values from -4 to 4, as said below
- qkv_bias: float32 [576], replicated, may hold values from -3 to 3
- proj_weight: bfloat16 [192, 192], replicated, may hold values from -0.4375 to 0.4375
Outputs:
- token_grad: bfloat16 [64, 32, 32, 192], P('gx', 'gy', 'gz')
- qkv_weight_grad: float32 [192, 576], replicated
- qkv_bias_grad: float32 [576], replicated
- proj_weight_grad: float32 [192, 192], replicated
- proj_bias_grad: float32 [192], replicated
- gain_grad: float32 [192], replicated
- norm_bias_grad: float32 [192], replicated
Inputs may be any that keep to these rules, and one draw needn't show every extreme that they name: `qkv_weight`: columns are the query, key and value projections in that order, each 6 heads of 32 columns.
All inputs are finite; a program needn't handle non-finite values.
Results may differ from a plain program's by a relative error of at most 0.02.
The roundings to bfloat16 on the way count: a program that leaves them out, or rounds other values in their place, can miss the bound.
Values may be sent and summed in bfloat16 or wider, within the bound.
A program may use at most 64 MiB of HBM per device.

v0:
```python
import jax
import jax.numpy as jnp
from jax import lax
from jax.sharding import PartitionSpec as P

HEADS = 6
WIN = 8
SHIFT = 4


def passed_along(value, axis, steps):
    count = lax.axis_size(axis)
    pairs = [(source, (source + steps) % count) for source in range(count)]
    return lax.ppermute(value, axis, pairs)


def window_grads(tok, upward, idents, norm_gain, norm_bias, qkv_weight, qkv_bias, proj_weight):
    length = tok.shape[0]
    width = tok.shape[1]
    heads = HEADS
    head_size = width // heads
    single = jnp.float32
    factor = head_size ** (-0.5)
    inputs = tok.astype(single)
    centred = inputs - jnp.mean(inputs, axis=-1, keepdims=True)
    inverse = lax.rsqrt(jnp.mean(centred * centred, axis=-1, keepdims=True) + 1e-05)
    normed = centred * inverse
    hidden = (normed * norm_gain + norm_bias).astype(jnp.bfloat16)
    packed = (jnp.dot(hidden, qkv_weight, preferred_element_type=single) + qkv_bias).astype(
        jnp.bfloat16
    )
    query = packed[:, :width].reshape(length, heads, head_size)
    keyset = packed[:, width : 2 * width].reshape(length, heads, head_size)
    valset = packed[:, 2 * width :].reshape(length, heads, head_size)
    scores = jnp.einsum("qhd,khd->hqk", query, keyset, preferred_element_type=single) * factor
    same = idents[:, None] == idents[None, :]
    scores = jnp.where(same[None], scores, -1e30)
    peak = jnp.max(scores, axis=-1, keepdims=True)
    expo = jnp.exp(scores - peak)
    probs = expo / jnp.sum(expo, axis=-1, keepdims=True)
    probs_half = probs.astype(jnp.bfloat16)
    attended = jnp.einsum("hqk,khd->qhd", probs_half, valset, preferred_element_type=single)
    attended = attended.reshape(length, width).astype(jnp.bfloat16)
    grad_proj = jnp.einsum("lc,lf->cf", attended, upward, preferred_element_type=single)
    grad_pbias = jnp.sum(upward.astype(single), axis=0)
    attended_grad = jnp.einsum(
        "lf,cf->lc", upward, proj_weight, preferred_element_type=single
    ).astype(jnp.bfloat16)
    attended_grad = attended_grad.reshape(length, heads, head_size)
    prob_grad = jnp.einsum("qhd,khd->hqk", attended_grad, valset, preferred_element_type=single)
    inner = jnp.sum(probs * prob_grad, axis=-1, keepdims=True)
    score_grad = (probs * (prob_grad - inner) * factor).astype(jnp.bfloat16)
    query_grad = jnp.einsum(
        "hqk,khd->qhd", score_grad, keyset, preferred_element_type=single
    ).reshape(length, width)
    key_grad = jnp.einsum("hqk,qhd->khd", score_grad, query, preferred_element_type=single).reshape(
        length, width
    )
    value_grad = jnp.einsum(
        "hqk,qhd->khd", probs_half, attended_grad, preferred_element_type=single
    ).reshape(length, width)
    packed_grad = jnp.concatenate([query_grad, key_grad, value_grad], axis=1).astype(jnp.bfloat16)
    grad_qkv = jnp.einsum("lc,lf->cf", hidden, packed_grad, preferred_element_type=single)
    grad_qbias = jnp.sum(packed_grad.astype(single), axis=0)
    hidden_grad = jnp.einsum("lf,cf->lc", packed_grad, qkv_weight, preferred_element_type=single)
    grad_gain = jnp.sum(hidden_grad * normed, axis=0)
    grad_nbias = jnp.sum(hidden_grad, axis=0)
    normed_grad = hidden_grad * norm_gain
    first = jnp.mean(normed_grad, axis=-1, keepdims=True)
    second = jnp.mean(normed_grad * normed, axis=-1, keepdims=True)
    token_grad = (upward.astype(single) + inverse * (normed_grad - first - normed * second)).astype(
        jnp.bfloat16
    )
    return (token_grad, (grad_qkv, grad_qbias, grad_proj, grad_pbias, grad_gain, grad_nbias))


def to_windows(block):
    sizes = block.shape[:3]
    rest = block.shape[3:]
    shaped = block.reshape(
        (sizes[0] // WIN, WIN, sizes[1] // WIN, WIN, sizes[2] // WIN, WIN) + rest
    )
    order = (0, 2, 4, 1, 3, 5) + tuple(range(6, 6 + len(rest)))
    return shaped.transpose(order).reshape((-1, WIN**3) + rest)


def from_windows(wins, first, second, third):
    rest = wins.shape[2:]
    shaped = wins.reshape((first // WIN, second // WIN, third // WIN, WIN, WIN, WIN) + rest)
    order = (0, 3, 1, 4, 2, 5) + tuple(range(6, 6 + len(rest)))
    return shaped.transpose(order).reshape((first, second, third) + rest)


def move_first(pieces):
    sent = passed_along((pieces[0][:SHIFT], pieces[1][:SHIFT]), "gx", -1)
    return (
        jnp.concatenate([pieces[0][SHIFT:], sent[0]], axis=0),
        jnp.concatenate([pieces[1][SHIFT:], sent[1]], axis=0),
    )


def move_second(pieces):
    sent = passed_along((pieces[0][:, :SHIFT], pieces[1][:, :SHIFT]), "gy", -1)
    return (
        jnp.concatenate([pieces[0][:, SHIFT:], sent[0]], axis=1),
        jnp.concatenate([pieces[1][:, SHIFT:], sent[1]], axis=1),
    )


def move_third(pieces):
    sent = passed_along((pieces[0][:, :, :SHIFT], pieces[1][:, :, :SHIFT]), "gz", -1)
    return (
        jnp.concatenate([pieces[0][:, :, SHIFT:], sent[0]], axis=2),
        jnp.concatenate([pieces[1][:, :, SHIFT:], sent[1]], axis=2),
    )


def window_index(count, position, length):
    total = length * count
    rolled = position * length + jnp.arange(length, dtype=jnp.int32)
    placed = (rolled + SHIFT) % total
    return ((placed + SHIFT) // WIN, total // WIN + 1, count)


def per_device(tokens, upstream, norm_gain, norm_bias, qkv_weight, qkv_bias, proj_weight):
    pieces = (tokens, upstream)
    pieces = move_third(move_second(move_first(pieces)))
    rolled, rolled_up = pieces
    depth_x, depth_y, depth_z, width = tokens.shape
    index_x, span_x, count_x = window_index(lax.axis_size("gx"), lax.axis_index("gx"), depth_x)
    index_y, span_y, count_y = window_index(lax.axis_size("gy"), lax.axis_index("gy"), depth_y)
    index_z, span_z, count_z = window_index(lax.axis_size("gz"), lax.axis_index("gz"), depth_z)
    idents = (index_x[:, None, None] * span_y + index_y[None, :, None]) * span_z + index_z[
        None, None, :
    ]
    token_wins = to_windows(rolled)
    up_wins = to_windows(rolled_up)
    ident_wins = to_windows(idents)
    zeros = (
        jnp.zeros((width, 3 * width), jnp.float32),
        jnp.zeros((3 * width,), jnp.float32),
        jnp.zeros((width, width), jnp.float32),
        jnp.zeros((width,), jnp.float32),
        jnp.zeros((width,), jnp.float32),
        jnp.zeros((width,), jnp.float32),
    )

    def advance(carry, item):
        grad_win, parts = window_grads(
            item[0], item[1], item[2], norm_gain, norm_bias, qkv_weight, qkv_bias, proj_weight
        )
        return (tuple((old + new for old, new in zip(carry, parts))), grad_win)

    totals, grad_wins = lax.scan(advance, zeros, (token_wins, up_wins, ident_wins))
    token_grad = from_windows(grad_wins, depth_x, depth_y, depth_z)
    summed = lax.psum(
        (totals[0], totals[1], totals[2], totals[3], totals[4], totals[5]), ("gx", "gy", "gz")
    )
    factor = float(depth_x * depth_y * depth_z * count_x * count_y * count_z) ** (-0.5)
    return (
        token_grad,
        summed[0] * factor,
        summed[1] * factor,
        summed[2] * factor,
        summed[3] * factor,
        summed[4] * factor,
        summed[5] * factor,
    )


def solution(mesh):
    placed = (P("gx", "gy", "gz", None), P("gx", "gy", "gz", None), P(), P(), P(), P(), P())
    return jax.shard_map(
        per_device,
        mesh=mesh,
        in_specs=placed,
        out_specs=(P("gx", "gy", "gz", None), P(), P(), P(), P(), P(), P()),
        check_vma=False,
    )
```

profile of v0, /device:TPU:0, one launch (start us, length us, event | category | flops | bytes accessed | tf_op | source)
XLA Modules:
  0.0 353.3 jit_solution(9239623265819939618)
XLA Ops:
  8.5 6.0 %collective-permute-start = (bf16[4,16,16,192]{3,2,1,0:T(8,128)(2,1)S(1)}, bf16[4,16,16,192]{3,2,1,0:T(8,128)(2,1)S(1)}, u32[]{:S(2)}, u32[]{:S(2)}) collective-permute-start(bf16[4,16,16,192]{3,2,1,0:T(8,128)(2,1)S(1)} %get-tuple-element.238), channel_id=1, source_target_pairs={{0,28},{4,0},{8,4},{12,8},{16,12},{20,16},{24,20},{28,24},{1,29},{... | collective-permute-start | bytes 1179656 | tf_op jit(solution)/shard_map/ppermute | solution.py:14
  16.9 10.0 %collective-permute-done = bf16[4,16,16,192]{3,2,1,0:T(8,128)(2,1)S(1)} collective-permute-done((bf16[4,16,16,192]{3,2,1,0:T(8,128)(2,1)S(1)}, bf16[4,16,16,192]{3,2,1,0:T(8,128)(2,1)S(1)}, u32[]{:S(2)}, u32[]{:S(2)}) %collective-permute-start) | collective-permute-done | bytes 393248 | tf_op jit(solution)/shard_map/ppermute | solution.py:14
  27.0 10.0 %collective-permute-done.3 = bf16[4,16,16,192]{3,2,1,0:T(8,128)(2,1)S(1)} collective-permute-done((bf16[4,16,16,192]{3,2,1,0:T(8,128)(2,1)S(1)}, bf16[4,16,16,192]{3,2,1,0:T(8,128)(2,1)S(1)}, u32[]{:S(2)}, u32[]{:S(2)}) %collective-permute-start.3) | collective-permute-done | bytes 393248 | tf_op jit(solution)/shard_map/ppermute | solution.py:14
  41.6 5.1 %collective-permute-done.2 = bf16[8,16,4,192]{3,2,1,0:T(4,128)(2,1)S(1)} collective-permute-done((bf16[8,16,4,192]{3,2,1,0:T(4,128)(2,1)S(1)}, bf16[8,16,4,192]{3,2,1,0:T(4,128)(2,1)S(1)}, u32[]{:S(2)}, u32[]{:S(2)}) %collective-permute-start.2) | collective-permute-done | bytes 196640 | tf_op jit(solution)/shard_map/ppermute | solution.py:14
  48.1 3.9 %collective-permute-done.5 = bf16[8,16,4,192]{3,2,1,0:T(4,128)(2,1)} collective-permute-done((bf16[8,16,4,192]{3,2,1,0:T(4,128)(2,1)}, bf16[8,16,4,192]{3,2,1,0:T(4,128)(2,1)}, u32[]{:S(2)}, u32[]{:S(2)}) %collective-permute-start.5) | collective-permute-done | bytes 196640 | tf_op jit(solution)/shard_map/ppermute | solution.py:14
  54.1 158.2 %while.23 = (s32[]{:T(128)}, f32[192,576]{1,0:T(8,128)S(1)}, f32[576]{0:T(1024)S(1)}, f32[192,192]{1,0:T(8,128)S(1)}, f32[192]{0:T(256)S(1)}, /*index=5*/f32[192...) while((s32[]{:T(128)}, f32[192,576]{1,0:T(8,128)S(1)}, ...), condition=%wide.region_12.13_spmd.clone, body=%wide.region_0.12_spmd.clone.sunk | while | flops 1065100416 | bytes 87224056 | solution.py:154
  56.2 5.1 %fusion.146 = (f32[6,512]{1,0:T(8,128)S(1)}, f32[6,512,512]{1,2,0:T(8,128)}) fusion(pred[512,512]{0,1:T(8,128)(4,1)S(1)} %broadcast_compare_fusion.2, bf16[512,6,32]{0,2,1:T(8,128)(2,1)S(1)} %bitcast.162, bf16[512,6,32]{0,2,1:T(8,128)(2,1)S(1)} %bitcast.164), kind=kOutput, calls=%fused_computation.127.clone.1 | convolution fusion | flops 106955264 | bytes 6959104 | tf_op jit(solution)/shard_map/while/body/eval_jaxpr/sub | solution.py:39
  67.0 3.7 %fusion.148 = f32[6,512,512]{1,2,0:T(8,128)} fusion(bf16[512,6,32]{0,2,1:T(8,128)(2,1)S(1)} %bitcast.161, bf16[512,6,32]{0,2,1:T(8,128)(2,1)S(1)} %bitcast.159), kind=kOutput, calls=%fused_computation.130.clone.1 | convolution fusion | flops 100663296 | bytes 6684672 | tf_op jit(solution)/shard_map/while/body/eval_jaxpr/qhd,khd->hqk/dot_general | solution.py:50
  70.7 10.8 %fusion.150 = bf16[6,32,512]{2,1,0:T(8,128)(2,1)S(1)} fusion(bf16[512,6,32]{0,2,1:T(8,128)(2,1)S(1)} %bitcast.165, f32[6,512,512]{1,2,0:T(8,128)} %fusion.148, f32[6,512,512]{1,2,0:T(8,128)} %get-tuple-element.353, f32[6,512]{1,0:T(8,128)S(1)} %get-tuple-element.354), kind=kOutput, calls=%fused_computation.22.clone.1 | convolution fusion | flops 111775232 | bytes 12988416 | tf_op jit(solution)/shard_map/while/body/eval_jaxpr/hqk,khd->qhd/dot_general | solution.py:53
  81.5 9.3 %fusion.149 = bf16[6,32,512]{2,1,0:T(8,128)(2,1)S(1)} fusion(bf16[512,6,32]{0,2,1:T(8,128)(2,1)S(1)} %bitcast.163, f32[6,512,512]{1,2,0:T(8,128)} %fusion.148, f32[6,512,512]{1,2,0:T(8,128)} %get-tuple-element.353, f32[6,512]{1,0:T(8,128)S(1)} %get-tuple-element.354), kind=kOutput, calls=%fused_computation.23.clone.1 | convolution fusion | flops 111775232 | bytes 12988416 | tf_op jit(solution)/shard_map/while/body/eval_jaxpr/hqk,qhd->khd/dot_general | solution.py:56
  95.8 5.1 %fusion.146 = (f32[6,512]{1,0:T(8,128)S(1)}, f32[6,512,512]{1,2,0:T(8,128)}) fusion(pred[512,512]{0,1:T(8,128)(4,1)S(1)} %broadcast_compare_fusion.2, bf16[512,6,32]{0,2,1:T(8,128)(2,1)S(1)} %bitcast.162, bf16[512,6,32]{0,2,1:T(8,128)(2,1)S(1)} %bitcast.164), kind=kOutput, calls=%fused_computation.127.clone.1 | convolution fusion | flops 106955264 | bytes 6959104 | tf_op jit(solution)/shard_map/while/body/eval_jaxpr/sub | solution.py:39
  106.5 3.7 %fusion.148 = f32[6,512,512]{1,2,0:T(8,128)} fusion(bf16[512,6,32]{0,2,1:T(8,128)(2,1)S(1)} %bitcast.161, bf16[512,6,32]{0,2,1:T(8,128)(2,1)S(1)} %bitcast.159), kind=kOutput, calls=%fused_computation.130.clone.1 | convolution fusion | flops 100663296 | bytes 6684672 | tf_op jit(solution)/shard_map/while/body/eval_jaxpr/qhd,khd->hqk/dot_general | solution.py:50
  110.2 10.8 %fusion.150 = bf16[6,32,512]{2,1,0:T(8,128)(2,1)S(1)} fusion(bf16[512,6,32]{0,2,1:T(8,128)(2,1)S(1)} %bitcast.165, f32[6,512,512]{1,2,0:T(8,128)} %fusion.148, f32[6,512,512]{1,2,0:T(8,128)} %get-tuple-element.353, f32[6,512]{1,0:T(8,128)S(1)} %get-tuple-element.354), kind=kOutput, calls=%fused_computation.22.clone.1 | convolution fusion | flops 111775232 | bytes 12988416 | tf_op jit(solution)/shard_map/while/body/eval_jaxpr/hqk,khd->qhd/dot_general | solution.py:53
  121.0 9.3 %fusion.149 = bf16[6,32,512]{2,1,0:T(8,128)(2,1)S(1)} fusion(bf16[512,6,32]{0,2,1:T(8,128)(2,1)S(1)} %bitcast.163, f32[6,512,512]{1,2,0:T(8,128)} %fusion.148, f32[6,512,512]{1,2,0:T(8,128)} %get-tuple-element.353, f32[6,512]{1,0:T(8,128)S(1)} %get-tuple-element.354), kind=kOutput, calls=%fused_computation.23.clone.1 | convolution fusion | flops 111775232 | bytes 12988416 | tf_op jit(solution)/shard_map/while/body/eval_jaxpr/hqk,qhd->khd/dot_general | solution.py:56
  135.3 5.1 %fusion.146 = (f32[6,512]{1,0:T(8,128)S(1)}, f32[6,512,512]{1,2,0:T(8,128)}) fusion(pred[512,512]{0,1:T(8,128)(4,1)S(1)} %broadcast_compare_fusion.2, bf16[512,6,32]{0,2,1:T(8,128)(2,1)S(1)} %bitcast.162, bf16[512,6,32]{0,2,1:T(8,128)(2,1)S(1)} %bitcast.164), kind=kOutput, calls=%fused_computation.127.clone.1 | convolution fusion | flops 106955264 | bytes 6959104 | tf_op jit(solution)/shard_map/while/body/eval_jaxpr/sub | solution.py:39
  146.1 3.7 %fusion.148 = f32[6,512,512]{1,2,0:T(8,128)} fusion(bf16[512,6,32]{0,2,1:T(8,128)(2,1)S(1)} %bitcast.161, bf16[512,6,32]{0,2,1:T(8,128)(2,1)S(1)} %bitcast.159), kind=kOutput, calls=%fused_computation.130.clone.1 | convolution fusion | flops 100663296 | bytes 6684672 | tf_op jit(solution)/shard_map/while/body/eval_jaxpr/qhd,khd->hqk/dot_general | solution.py:50
  149.8 10.8 %fusion.150 = bf16[6,32,512]{2,1,0:T(8,128)(2,1)S(1)} fusion(bf16[512,6,32]{0,2,1:T(8,128)(2,1)S(1)} %bitcast.165, f32[6,512,512]{1,2,0:T(8,128)} %fusion.148, f32[6,512,512]{1,2,0:T(8,128)} %get-tuple-element.353, f32[6,512]{1,0:T(8,128)S(1)} %get-tuple-element.354), kind=kOutput, calls=%fused_computation.22.clone.1 | convolution fusion | flops 111775232 | bytes 12988416 | tf_op jit(solution)/shard_map/while/body/eval_jaxpr/hqk,khd->qhd/dot_general | solution.py:53
  160.6 9.3 %fusion.149 = bf16[6,32,512]{2,1,0:T(8,128)(2,1)S(1)} fusion(bf16[512,6,32]{0,2,1:T(8,128)(2,1)S(1)} %bitcast.163, f32[6,512,512]{1,2,0:T(8,128)} %fusion.148, f32[6,512,512]{1,2,0:T(8,128)} %get-tuple-element.353, f32[6,512]{1,0:T(8,128)S(1)} %get-tuple-element.354), kind=kOutput, calls=%fused_computation.23.clone.1 | convolution fusion | flops 111775232 | bytes 12988416 | tf_op jit(solution)/shard_map/while/body/eval_jaxpr/hqk,qhd->khd/dot_general | solution.py:56
  174.9 5.1 %fusion.146 = (f32[6,512]{1,0:T(8,128)S(1)}, f32[6,512,512]{1,2,0:T(8,128)}) fusion(pred[512,512]{0,1:T(8,128)(4,1)S(1)} %broadcast_compare_fusion.2, bf16[512,6,32]{0,2,1:T(8,128)(2,1)S(1)} %bitcast.162, bf16[512,6,32]{0,2,1:T(8,128)(2,1)S(1)} %bitcast.164), kind=kOutput, calls=%fused_computation.127.clone.1 | convolution fusion | flops 106955264 | bytes 6959104 | tf_op jit(solution)/shard_map/while/body/eval_jaxpr/sub | solution.py:39
  185.6 3.7 %fusion.148 = f32[6,512,512]{1,2,0:T(8,128)} fusion(bf16[512,6,32]{0,2,1:T(8,128)(2,1)S(1)} %bitcast.161, bf16[512,6,32]{0,2,1:T(8,128)(2,1)S(1)} %bitcast.159), kind=kOutput, calls=%fused_computation.130.clone.1 | convolution fusion | flops 100663296 | bytes 6684672 | tf_op jit(solution)/shard_map/while/body/eval_jaxpr/qhd,khd->hqk/dot_general | solution.py:50
  189.3 10.8 %fusion.150 = bf16[6,32,512]{2,1,0:T(8,128)(2,1)S(1)} fusion(bf16[512,6,32]{0,2,1:T(8,128)(2,1)S(1)} %bitcast.165, f32[6,512,512]{1,2,0:T(8,128)} %fusion.148, f32[6,512,512]{1,2,0:T(8,128)} %get-tuple-element.353, f32[6,512]{1,0:T(8,128)S(1)} %get-tuple-element.354), kind=kOutput, calls=%fused_computation.22.clone.1 | convolution fusion | flops 111775232 | bytes 12988416 | tf_op jit(solution)/shard_map/while/body/eval_jaxpr/hqk,khd->qhd/dot_general | solution.py:53
  200.1 9.3 %fusion.149 = bf16[6,32,512]{2,1,0:T(8,128)(2,1)S(1)} fusion(bf16[512,6,32]{0,2,1:T(8,128)(2,1)S(1)} %bitcast.163, f32[6,512,512]{1,2,0:T(8,128)} %fusion.148, f32[6,512,512]{1,2,0:T(8,128)} %get-tuple-element.353, f32[6,512]{1,0:T(8,128)S(1)} %get-tuple-element.354), kind=kOutput, calls=%fused_computation.23.clone.1 | convolution fusion | flops 111775232 | bytes 12988416 | tf_op jit(solution)/shard_map/while/body/eval_jaxpr/hqk,qhd->khd/dot_general | solution.py:56
  213.2 40.9 %all-reduce = (f32[576]{0:T(1024)S(1)}, f32[192]{0:T(256)S(1)}, f32[192]{0:T(256)S(1)}, f32[192]{0:T(256)S(1)}) all-reduce(f32[576]{0:T(1024)S(1)} %get-tuple-element.97, f32[192]{0:T(256)S(1)} %get-tuple-element.99, f32[192]{0:T(256)S(1)} %get-tuple-element.100, ...), channel_id=1, replica_groups=mesh['gx'=8,'gy'=2,'gz'=2] {'gx','gy','gz'}, use_global_device_ids=true, to_apply=%region_14.15 | all-reduce | flops 1152 | bytes 9216 | tf_op jit(solution)/shard_map/psum | solution.py:156
  258.3 84.7 %all-reduce.4.cloned.1.call-done = (f32[192,576]{1,0:T(8,128)}, f32[192,192]{1,0:T(8,128)}) async-done(((f32[192,576]{1,0:T(8,128)}, f32[192,192]{1,0:T(8,128)}), (f32[192,576]{1,0:T(8,128)}, f32[192,192]{1,0:T(8,128)})) %all-reduce.4.cloned.1.call-update) | async-done | bytes 589840 | tf_op jit(solution)/shard_map/psum | solution.py:156
  (155 shorter events, 62.7 us)
Async XLA Ops:
  7.2 335.8 %all-reduce.4.cloned.1.call-start = ((), (), s32[]{:S(2)}) async-start(), calls=%async_computation | async-start | bytes 1376256 | tf_op jit(solution)/shard_map/psum | solution.py:156
  8.5 18.4 %collective-permute-start = (bf16[4,16,16,192]{3,2,1,0:T(8,128)(2,1)S(1)}, bf16[4,16,16,192]{3,2,1,0:T(8,128)(2,1)S(1)}, u32[]{:S(2)}, u32[]{:S(2)}) collective-permute-start(bf16[4,16,16,192]{3,2,1,0:T(8,128)(2,1)S(1)} %get-tuple-element.238), channel_id=1, source_target_pairs={{0,28},{4,0},{8,4},{12,8},{16,12},{20,16},{24,20},{28,24},{1,29},{... | collective-permute-start | bytes 1179656 | tf_op jit(solution)/shard_map/ppermute | solution.py:14
  15.9 21.1 %collective-permute-start.3 = (bf16[4,16,16,192]{3,2,1,0:T(8,128)(2,1)S(1)}, bf16[4,16,16,192]{3,2,1,0:T(8,128)(2,1)S(1)}, u32[]{:S(2)}, u32[]{:S(2)}) collective-permute-start(bf16[4,16,16,192]{3,2,1,0:T(8,128)(2,1)S(1)} %get-tuple-element.236), channel_id=1, source_target_pairs={{0,28},{4,0},{8,4},{12,8},{16,12},{20,16},{24,20},{28,24},{1,29},{... | collective-permute-start | bytes 1179656 | tf_op jit(solution)/shard_map/ppermute | solution.py:14
  26.9 10.5 %collective-permute-start.1 = (bf16[8,4,16,192]{3,2,1,0:T(8,128)(2,1)S(1)}, bf16[8,4,16,192]{3,2,1,0:T(8,128)(2,1)S(1)}, u32[]{:S(2)}, u32[]{:S(2)}) collective-permute-start(bf16[8,4,16,192]{3,2,1,0:T(8,128)(2,1)S(1)} %pad_maximum_fusion.8), channel_id=1, source_target_pairs={{0,2},{2,0},{1,3},{3,1},{4,6},{6,4},{5,7},{7,5},{8,10},{10,8},{9,1... | collective-permute-start | bytes 589832 | tf_op jit(solution)/shard_map/ppermute | solution.py:14
  37.0 2.1 collective-permute-start.4
  37.5 9.2 %collective-permute-start.2 = (bf16[8,16,4,192]{3,2,1,0:T(4,128)(2,1)S(1)}, bf16[8,16,4,192]{3,2,1,0:T(4,128)(2,1)S(1)}, u32[]{:S(2)}, u32[]{:S(2)}) collective-permute-start(bf16[8,16,4,192]{3,2,1,0:T(4,128)(2,1)S(1)} %pad_maximum_fusion.7), channel_id=1, source_target_pairs={{0,1},{1,0},{2,3},{3,2},{4,5},{5,4},{6,7},{7,6},{8,9},{9,8},{10,11... | collective-permute-start | bytes 589832 | tf_op jit(solution)/shard_map/ppermute | solution.py:14
  39.9 12.1 %collective-permute-start.5 = (bf16[8,16,4,192]{3,2,1,0:T(4,128)(2,1)}, bf16[8,16,4,192]{3,2,1,0:T(4,128)(2,1)}, u32[]{:S(2)}, u32[]{:S(2)}) collective-permute-start(bf16[8,16,4,192]{3,2,1,0:T(4,128)(2,1)} %pad_maximum_fusion.5), channel_id=1, source_target_pairs={{0,1},{1,0},{2,3},{3,2},{4,5},{5,4},{6,7},{7,6},{8,9},{9,8},{10,11... | collective-permute-start | bytes 589832 | tf_op jit(solution)/shard_map/ppermute | solution.py:14
  41.6 12.5 %copy-start.1 = (bf16[192,192]{1,0:T(8,128)(2,1)S(1)}, bf16[192,192]{1,0:T(8,128)(2,1)}, u32[]{:S(2)}) copy-start(bf16[192,192]{1,0:T(8,128)(2,1)} %param.15) | copy-start | bytes 221188
  41.6 12.5 %copy-start.4 = (f32[192]{0:T(256)S(1)}, f32[192]{0:T(256)}, u32[]{:S(2)}) copy-start(f32[192]{0:T(256)} %param.11) | copy-start | bytes 2308
  41.6 12.5 %copy-start.5 = (f32[576]{0:T(1024)S(1)}, f32[576]{0:T(1024)}, u32[]{:S(2)}) copy-start(f32[576]{0:T(1024)} %param.14) | copy-start | bytes 6916
  41.6 12.5 %copy-start.6 = (f32[192]{0:T(256)S(1)}, f32[192]{0:T(256)}, u32[]{:S(2)}) copy-start(f32[192]{0:T(256)} %param.12) | copy-start | bytes 2308
  48.0 6.1 %copy-start.2 = (f32[192,576]{1,0:T(8,128)S(1)}, f32[192,576]{1,0:T(8,128)}, u32[]{:S(2)}) copy-start(f32[192,576]{1,0:T(8,128)} %custom-call) | copy-start | bytes 1327108
  61.3 4.6 %copy-start.7 = (f32[6,512,512]{1,2,0:T(8,128)S(1)}, f32[6,512,512]{1,2,0:T(8,128)}, u32[]{:S(2)}) copy-start(f32[6,512,512]{1,2,0:T(8,128)} %get-tuple-element.353) | copy-start | bytes 18874372 | tf_op jit(solution)/shard_map/while
  100.9 4.6 %copy-start.7 = (f32[6,512,512]{1,2,0:T(8,128)S(1)}, f32[6,512,512]{1,2,0:T(8,128)}, u32[]{:S(2)}) copy-start(f32[6,512,512]{1,2,0:T(8,128)} %get-tuple-element.353) | copy-start | bytes 18874372 | tf_op jit(solution)/shard_map/while
  140.4 4.6 %copy-start.7 = (f32[6,512,512]{1,2,0:T(8,128)S(1)}, f32[6,512,512]{1,2,0:T(8,128)}, u32[]{:S(2)}) copy-start(f32[6,512,512]{1,2,0:T(8,128)} %get-tuple-element.353) | copy-start | bytes 18874372 | tf_op jit(solution)/shard_map/while
  180.0 4.6 %copy-start.7 = (f32[6,512,512]{1,2,0:T(8,128)S(1)}, f32[6,512,512]{1,2,0:T(8,128)}, u32[]{:S(2)}) copy-start(f32[6,512,512]{1,2,0:T(8,128)} %get-tuple-element.353) | copy-start | bytes 18874372 | tf_op jit(solution)/shard_map/while
  212.3 0.7 copy-start
  212.3 0.8 copy-start.3
Sparse Core Ops, SparseCore 0:
  213.3 129.5 all-reduce.3
where the time goes:
time: 354 us; the launch traced here: 353 us
  matrix products  149 us (42%)
  waiting for transfers between devices  114 us (32%)
  blocking collectives  40.9 us (12%)
  other arithmetic  15.2 us (4%)
  between operations  14.3 us (4%)
  local copies, waits for them, and re-layouts  10.6 us (3%)
  starting transfers between devices  9.45 us (3%)
    psum x1, waiting for transfers between devices, per_device(): lax.psum((totals[0], totals[1], totals[2], totals[3], totals[4], totals[5...  84.7 us
    dot_general x4, matrix products, window_grads(): jnp.einsum('hqk,khd->qhd', score_grad, keyset, preferred_element_type=sin...  43.1 us
    psum x1, blocking collectives, per_device(): lax.psum((totals[0], totals[1], totals[2], totals[3], totals[4], totals[5...  40.9 us
    dot_general x4, matrix products, window_grads(): jnp.einsum('hqk,qhd->khd', score_grad, query, preferred_element_type=single)  37 us
    ppermute x6, waiting for transfers between devices, passed_along(): return lax.ppermute(value, axis, pairs)  29 us
    sub x4, matrix products, window_grads(): expo = jnp.exp(scores - peak)  20.4 us
    dot_general x4, matrix products, window_grads(): jnp.einsum('qhd,khd->hqk', attended_grad, valset, preferred_element_type=...  14.8 us
    dot_general x4, matrix products, window_grads(): jnp.einsum('hqk,khd->qhd', probs_half, valset, preferred_element_type=sin...  14.3 us
  transfers between devices with their start and end apart: 7, of which 5 were waited for; matrix products, arithmetic and copies ran while one was open for 3% of the time, Pallas kernels for 0%

commit v1 on v0

v1 whole, which is shorter than its diff:
```python
import functools

import jax
import jax.numpy as jnp
from jax import lax
from jax.experimental import pallas as pl
from jax.experimental.pallas import tpu as pltpu
from jax.sharding import PartitionSpec as P

HEADS = 6
WIN = 8
SHIFT = 4
CELL = SHIFT**3
LANES = 128
MASKED = -1e30
MESH = pl.DeviceIdType.MESH


def dot(left, right):
    return jnp.dot(left, right, preferred_element_type=jnp.float32)


def dot_nt(left, right):
    return lax.dot_general(
        left, right, (((1,), (1,)), ((), ())), preferred_element_type=jnp.float32
    )


def wrapped(value, size):
    return lax.rem(value + size, size)


def rows_at(start, size):
    return pl.ds(pl.multiple_of(start, 16), size)


def cell_order(cells_y, cells_z):
    area = SHIFT * SHIFT
    count = cells_y * cells_z * area
    row = lax.broadcasted_iota(jnp.int32, (count, count), 0)
    column = lax.broadcasted_iota(jnp.int32, (count, count), 1)
    cell, inside = row // area, row % area
    y = cell // cells_z * SHIFT + inside // SHIFT
    z = cell % cells_z * SHIFT + inside % SHIFT
    return jnp.where(column == y * (cells_z * SHIFT) + z, 1.0, 0.0).astype(jnp.bfloat16)


def kernel(
    counts, width, scale, tok_ref, upw_ref, gain_ref, nbias_ref, wt_ref, w_ref, qbias_ref, pw_ref,
    out_ref, qgrad_ref, qbgrad_ref, pgrad_ref, small_ref,
    cells_ref, wins_ref, res_ref, hid_ref, normed_ref, inv_ref, pk_ref, da_ref, att_ref, pg_ref,
    accq_ref, accp_ref, accs_ref, g_ref, tot_ref, first_ref, got_ref, mine_ref, parts_ref,
    send_sem, recv_sem, local_sem, pair_send, pair_recv, send2, recv2, send3, recv3,
):
    axes = ("gx", "gy", "gz")
    here = [lax.axis_index(axis) for axis in axes]
    sizes = [lax.axis_size(axis) for axis in axes]
    devices = sizes[0] * sizes[1] * sizes[2]
    chips = sizes[0] * sizes[2]
    core = here[1]
    me = here[0] * sizes[2] + here[2]
    spread = [count // 2 for count in counts]
    cells = counts[0] * counts[1] * counts[2]
    length = WIN**3
    area = SHIFT * SHIFT
    plane = counts[1] * counts[2] * area
    head = width // HEADS
    factor = head ** (-0.5)
    single = jnp.float32
    half = jnp.bfloat16

    barrier = pltpu.get_barrier_semaphore()
    rank = (here[0] * sizes[1] + here[1]) * sizes[2] + here[2]

    def greet(step, carry):
        other = lax.rem(rank + step, devices)
        place = {
            "gx": other // (sizes[1] * sizes[2]),
            "gy": lax.rem(other // sizes[2], sizes[1]),
            "gz": lax.rem(other, sizes[2]),
        }
        pl.semaphore_signal(barrier, inc=1, device_id=place, device_id_type=MESH)
        return carry

    lax.fori_loop(1, devices, greet, 0)

    order = cell_order(counts[1], counts[2])
    for x in range(counts[0] * SHIFT):
        inside = slice(x % SHIFT * area, (x % SHIFT + 1) * area)
        for source, lanes in ((tok_ref, slice(0, width)), (upw_ref, slice(width, 2 * width))):
            moved = dot(order, source[x].reshape(plane, width)).astype(half)
            cells_ref[x // SHIFT, :, inside, lanes] = moved.reshape(-1, area, width)
    pl.semaphore_wait(barrier, devices - 1)

    arriving = {}
    for a in range(counts[0]):
        for b in range(counts[1]):
            for c in range(counts[2]):
                offset = tuple(int(at == 0) for at in (a, b, c))
                to = [(at - 1) % count for at, count in zip((a, b, c), counts)]
                window = (to[0] // 2 * spread[1] + to[1] // 2) * spread[2] + to[2] // 2
                octant = (to[0] % 2 * 2 + to[1] % 2) * 2 + to[2] % 2
                number = window * 8 + octant
                source = cells_ref.at[a, b * counts[2] + c]
                target = wins_ref.at[window, octant]
                if any(offset):
                    copy = pltpu.make_async_remote_copy(
                        src_ref=source,
                        dst_ref=target,
                        send_sem=send_sem.at[number],
                        recv_sem=recv_sem.at[number],
                        device_id={
                            axis: wrapped(at - step, size)
                            for axis, at, step, size in zip(axes, here, offset, sizes)
                        },
                        device_id_type=MESH,
                    )
                else:
                    copy = pltpu.make_async_copy(source, target, local_sem.at[number])
                arriving[number] = (copy, any(offset))
    for number in sorted(arriving):
        arriving[number][0].start()

    hid_ref[...] = jnp.ones_like(hid_ref)
    accq_ref[...] = jnp.zeros_like(accq_ref)
    accp_ref[...] = jnp.zeros_like(accp_ref)
    accs_ref[...] = jnp.zeros_like(accs_ref)
    tile = min(256, length)
    exponent = factor * 1.4426950408889634

    def one_window(step, nothing):
        for window in range(cells // 8):

            @pl.when(step == window)
            def _():
                for octant in range(8):
                    copy, remote = arriving[window * 8 + octant]
                    if remote:
                        copy.wait_recv()
                    else:
                        copy.wait()

        both = wins_ref[step].reshape(length, 2 * width)
        inputs = both[:, :width].astype(single)
        up = both[:, width:]
        centred = inputs - jnp.mean(inputs, axis=-1, keepdims=True)
        inverse = lax.rsqrt(jnp.mean(centred * centred, axis=-1, keepdims=True) + 1e-05)
        normed = centred * inverse
        normed_ref[...] = normed
        inv_ref[...] = inverse
        hidden = (normed * gain_ref[...] + nbias_ref[...]).astype(half)
        hid_ref[:, :width] = hidden
        pk_ref[...] = (dot_nt(wt_ref[...], hidden) + qbias_ref[...]).astype(half)
        da_ref[...] = dot_nt(pw_ref[...], up).astype(half)

        place = (step // (spread[1] * spread[2]), step // spread[2] % spread[1], step % spread[2])
        cut = [
            jnp.where((at == size - 1) & (mine == count - 1), 1, 0)
            for at, size, mine, count in zip(here, sizes, place, spread)
        ]
        octants = lax.broadcasted_iota(jnp.int32, (16, length), 1) // CELL
        region = octants & (cut[0] * 4 + cut[1] * 2 + cut[2])
        own = region == lax.broadcasted_iota(jnp.int32, (16, length), 0)
        mark_q = jnp.where(own, 1.0, 0.0).astype(half)
        mark_k = jnp.where(own, 0.0, MASKED).astype(half)

        def one_head(h, carry):
            base = pl.multiple_of(h * head, head)
            qt = pk_ref[pl.ds(base, head), :]
            kt = pk_ref[pl.ds(base + width, head), :]
            vt = pk_ref[pl.ds(base + 2 * width, head), :]
            dat = da_ref[pl.ds(base, head), :]
            qt_marked = jnp.concatenate([qt, mark_q], axis=0)
            keys = jnp.concatenate([kt, mark_k], axis=0).T
            values = vt.T
            kg = jnp.zeros((head, length), single)
            vg = jnp.zeros((head, length), single)
            for start in range(0, length, tile):
                part = slice(start, start + tile)
                scores = dot(keys, qt_marked[:, part])
                prob_grad = dot(values, dat[:, part])
                peak = jnp.max(scores, axis=0, keepdims=True)
                expo = jnp.exp2((scores - peak) * exponent)
                probs = expo * (1.0 / jnp.sum(expo, axis=0, keepdims=True))
                inner = jnp.sum(probs * prob_grad, axis=0, keepdims=True)
                probs_half = probs.astype(half)
                score_grad = (probs * (prob_grad - inner)).astype(half)
                att_ref[pl.ds(base, head), part] = dot(vt, probs_half).astype(half)
                pg_ref[pl.ds(base, head), part] = (dot(kt, score_grad) * factor).astype(half)
                vg += dot_nt(dat[:, part], probs_half)
                kg += dot_nt(qt[:, part], score_grad)
            pg_ref[pl.ds(base + width, head), :] = (kg * factor).astype(half)
            pg_ref[pl.ds(base + 2 * width, head), :] = vg.astype(half)
            return carry

        lax.fori_loop(0, HEADS, one_head, 0, unroll=1)

        accq_ref[...] += dot(pg_ref[...], hid_ref[...])
        accp_ref[...] += dot(att_ref[...], up)
        hidden_grad = dot(w_ref[...], pg_ref[...]).T
        normed = normed_ref[...]
        up_single = up.astype(single)
        accs_ref[0:1, :] += jnp.sum(up_single, axis=0, keepdims=True)
        accs_ref[1:2, :] += jnp.sum(hidden_grad * normed, axis=0, keepdims=True)
        accs_ref[2:3, :] += jnp.sum(hidden_grad, axis=0, keepdims=True)
        normed_grad = hidden_grad * gain_ref[...]
        first = jnp.mean(normed_grad, axis=-1, keepdims=True)
        second = jnp.mean(normed_grad * normed, axis=-1, keepdims=True)
        token_grad = up_single + inv_ref[...] * (normed_grad - first - normed * second)
        res_ref[step] = token_grad.astype(half).reshape(8, CELL, width)
        return nothing

    lax.fori_loop(0, cells // 8, one_window, 0)

    total_rows = g_ref.shape[0]
    rest = width - LANES
    low = 4 * width
    last = slice(low + 3 * width, 2 * low)
    if total_rows > 2 * low:
        g_ref[2 * low :, :] = jnp.zeros((total_rows - 2 * low, LANES), single)
    g_ref[: 3 * width, :] = accq_ref[:, :LANES]
    g_ref[3 * width : low, :] = accp_ref[:, :LANES]
    g_ref[low : low + 3 * width, :] = accq_ref[:, LANES:]
    g_ref[last, :] = jnp.zeros((width, LANES), single)
    g_ref[last, :rest] = accp_ref[:, LANES:]
    g_ref[last, rest : rest + 8] = accs_ref[...].T

    middle = total_rows // 2
    chunk = middle // chips
    pair = {"gy": 1 - core}

    def chip(step):
        other = lax.rem(me + step, chips)
        return other, {"gx": other // sizes[2], "gz": lax.rem(other, sizes[2])}

    first_ref[...] = (g_ref[rows_at((1 - core) * middle, middle), :] * scale).astype(half)
    swap = pltpu.make_async_remote_copy(
        src_ref=first_ref, dst_ref=got_ref, send_sem=pair_send.at[0], recv_sem=pair_recv.at[0],
        device_id=pair, device_id_type=MESH,
    )
    swap.start()
    for number in sorted(arriving):
        if arriving[number][1]:
            arriving[number][0].wait_send()
    swap.wait()
    mine_ref[...] = (
        g_ref[rows_at(core * middle, middle), :] * scale + got_ref[...].astype(single)
    ).astype(half)

    def scatter(step):
        other, device = chip(step)
        return pltpu.make_async_remote_copy(
            src_ref=mine_ref.at[rows_at(other * chunk, chunk), :],
            dst_ref=parts_ref.at[step],
            send_sem=send2.at[step], recv_sem=recv2.at[step],
            device_id=device, device_id_type=MESH,
        )

    def start_scatter(step, carry):
        scatter(step).start()
        return carry

    def wait_scatter(step, carry):
        scatter(step).wait()
        return carry

    lax.fori_loop(1, chips, start_scatter, 0)

    def put_back(first_x, last_x):
        for x in range(first_x, last_x):
            inside = slice(x % SHIFT * area, (x % SHIFT + 1) * area)
            pieces = []
            for b in range(counts[1]):
                for c in range(counts[2]):
                    a = x // SHIFT
                    window = (a // 2 * spread[1] + b // 2) * spread[2] + c // 2
                    octant = (a % 2 * 2 + b % 2) * 2 + c % 2
                    pieces.append(res_ref[window, octant, inside, :])
            moved = lax.dot_general(
                order, jnp.concatenate(pieces, axis=0), (((0,), (0,)), ((), ())),
                preferred_element_type=single,
            )
            out_ref[x] = moved.astype(half).reshape(out_ref.shape[1:])

    planes = counts[0] * SHIFT
    put_back(0, planes // 2)
    lax.fori_loop(1, chips, wait_scatter, 0)
    parts_ref[0] = mine_ref[rows_at(me * chunk, chunk), :]
    spot = rows_at(core * middle + me * chunk, chunk)

    def add(step, total):
        return total + parts_ref[step].astype(single)

    total = lax.fori_loop(0, chips, add, jnp.zeros((chunk, LANES), single))
    tot_ref[spot, :] = total.astype(half)

    def gather(step):
        return pltpu.make_async_remote_copy(
            src_ref=tot_ref.at[spot, :],
            dst_ref=tot_ref.at[spot, :],
            send_sem=send3.at[step], recv_sem=recv3.at[step],
            device_id=chip(step)[1], device_id_type=MESH,
        )

    def start_gather(step, carry):
        gather(step).start()
        return carry

    def wait_gather(step, carry):
        gather(step).wait()
        return carry

    lax.fori_loop(1, chips, start_gather, 0)
    put_back(planes // 2, planes)
    lax.fori_loop(1, chips, wait_gather, 0)
    final = rows_at(core * middle, middle)
    swap = pltpu.make_async_remote_copy(
        src_ref=tot_ref.at[final, :], dst_ref=tot_ref.at[final, :],
        send_sem=pair_send.at[1], recv_sem=pair_recv.at[1],
        device_id=pair, device_id_type=MESH,
    )
    swap.start()
    swap.wait()
    qgrad_ref[:LANES, :] = tot_ref[: 3 * width, :].astype(single).T
    high = tot_ref[low : low + 3 * width, :].astype(single).T
    qgrad_ref[LANES:, :] = high[:rest]
    qbgrad_ref[...] = high[rest : rest + 1]
    ends = tot_ref[last, :].astype(single)
    pgrad_ref[:, :LANES] = tot_ref[3 * width : low, :].astype(single)
    pgrad_ref[:, LANES:] = ends[:, :rest]
    small_ref[...] = ends.T[rest : rest + 8]


def per_device(tokens, upstream, norm_gain, norm_bias, qkv_weight, qkv_bias, proj_weight):
    x, y, z, width = tokens.shape
    chips = lax.axis_size("gx") * lax.axis_size("gz")
    devices = chips * lax.axis_size("gy")
    counts = (x // SHIFT, y // SHIFT, z // SHIFT)
    cells = counts[0] * counts[1] * counts[2]
    length = WIN**3
    step = 16 * devices
    rows = -(-8 * width // step) * step
    middle = rows // 2
    scale = float(x * y * z * devices) ** (-0.5)
    vmem = pl.BlockSpec(memory_space=pltpu.VMEM)
    half = jnp.bfloat16
    single = jnp.float32
    dma = pltpu.SemaphoreType.DMA
    token_grad, qgrad, qbgrad, pgrad, small = pl.pallas_call(
        functools.partial(kernel, counts, width, scale),
        out_shape=(
            jax.ShapeDtypeStruct(tokens.shape, half),
            jax.ShapeDtypeStruct((width, 3 * width), single),
            jax.ShapeDtypeStruct((1, 3 * width), single),
            jax.ShapeDtypeStruct((width, width), single),
            jax.ShapeDtypeStruct((8, width), single),
        ),
        in_specs=[vmem] * 8,
        out_specs=(vmem,) * 5,
        scratch_shapes=[
            pltpu.VMEM((counts[0], counts[1] * counts[2], CELL, 2 * width), half),
            pltpu.VMEM((cells // 8, 8, CELL, 2 * width), half),
            pltpu.VMEM((cells // 8, 8, CELL, width), half),
            pltpu.VMEM((length, 2 * LANES), half),
            pltpu.VMEM((length, width), single),
            pltpu.VMEM((length, 1), single),
            pltpu.VMEM((3 * width, length), half),
            pltpu.VMEM((width, length), half),
            pltpu.VMEM((width, length), half),
            pltpu.VMEM((3 * width, length), half),
            pltpu.VMEM((3 * width, 2 * LANES), single),
            pltpu.VMEM((width, width), single),
            pltpu.VMEM((8, width), single),
            pltpu.VMEM((rows, LANES), single),
            pltpu.VMEM((rows, LANES), half),
            pltpu.VMEM((middle, LANES), half),
            pltpu.VMEM((middle, LANES), half),
            pltpu.VMEM((middle, LANES), half),
            pltpu.VMEM((chips, middle // chips, LANES), half),
            dma((cells,)),
            dma((cells,)),
            dma((cells,)),
            dma((2,)),
            dma((2,)),
            dma((chips,)),
            dma((chips,)),
            dma((chips,)),
            dma((chips,)),
        ],
        compiler_params=pltpu.CompilerParams(
            collective_id=0, has_side_effects=True, vmem_limit_bytes=48 * 1024 * 1024
        ),
    )(
        tokens,
        upstream,
        norm_gain.reshape(1, width),
        norm_bias.reshape(1, width),
        qkv_weight.T,
        qkv_weight,
        qkv_bias.reshape(3 * width, 1),
        proj_weight,
    )
    return (token_grad, qgrad, qbgrad[0], pgrad, small[0], small[1], small[2])


def solution(mesh):
    placed = (P("gx", "gy", "gz", None), P("gx", "gy", "gz", None), P(), P(), P(), P(), P())
    return jax.shard_map(
        per_device,
        mesh=mesh,
        in_specs=placed,
        out_specs=(P("gx", "gy", "gz", None), P(), P(), P(), P(), P(), P()),
        check_vma=False,
    )
```

time: 354 us -> 82.1 us (0.23)
  matrix products: 149 us -> 0 us
  waiting for transfers between devices: 114 us -> 0 us
  Pallas kernels: 0 us -> 73.1 us
  blocking collectives: 40.9 us -> 0 us
  other arithmetic: 15.2 us -> 0.6 us
  between operations: 14.3 us -> 0.71 us
  starting transfers between devices: 9.45 us -> 0 us
    dot_general x40 -> x0, matrix products: 128 us -> none  [the longest x4 43.1 us: window_grads(): jnp.einsum('hqk,khd->qhd', score_grad, keyset, preferred_element_type=sin...]
    psum x1 -> x0, waiting for transfers between devices: 84.7 us -> none  [per_device(): lax.psum((totals[0], totals[1], totals[2], totals[3], totals[4], totals[5...]
    pallas_call x0 -> x1, Pallas kernels: none -> 73.1 us  [per_device(): pl.pallas_call(functools.partial(kernel, counts, width, scale), out_shape...]
    psum x1 -> x0, blocking collectives: 40.9 us -> none  [per_device(): lax.psum((totals[0], totals[1], totals[2], totals[3], totals[4], totals[5...]
    ppermute x6 -> x0, waiting for transfers between devices: 29 us -> none  [passed_along(): return lax.ppermute(value, axis, pairs)]
    sub x4 -> x0, matrix products: 20.4 us -> none  [window_grads(): expo = jnp.exp(scores - peak)]
    ppermute x6 -> x0, starting transfers between devices: 9.41 us -> none  [passed_along(): return lax.ppermute(value, axis, pairs)]
    mul x7 -> x0, other arithmetic: 5.28 us -> none  [the longest x1 1.84 us: per_device(): summed[0] * factor]
  transfers between devices with their start and end apart: 7 -> 0, of which waited for: 5 -> 0; matrix products, arithmetic and copies ran while one was open for 3% -> 0% of each run, Pallas kernels for 0% -> 0%
where the time goes in v1:
time: 82.1 us; the launch traced here: 81.9 us
  Pallas kernels  73.1 us (89%)
  local copies, waits for them, and re-layouts  7.49 us (9%)
    pallas_call x1, Pallas kernels, per_device(): pl.pallas_call(functools.partial(kernel, counts, width, scale), out_shape...  73.1 us
    unnamed x18, local copies, waits for them, and re-layouts  6.78 us

profile of v1, /device:TPU:0, one launch (start us, length us, event | category | flops | bytes accessed | tf_op | source)
XLA Modules:
  0.0 81.9 jit_solution(10549227881057496621)
XLA Ops:
  0.6 0.0 copy-start.6
  0.6 0.0 copy-start.3
  0.7 1.1 %copy.15 = bf16[192,576]{0,1:T(8,128)(2,1)S(1)} copy(bf16[192,576]{1,0:T(8,128)(2,1)} %w_ref.1) | data formatting | bytes 442368 | tf_op args[4]
  1.8 0.0 copy-start.2
  1.8 0.0 copy-done.6
  1.8 0.0 copy-start.5
  1.8 0.1 reshape.26.qbias_ref
  2.0 0.0 copy-start.4
  2.0 0.0 copy-done.3
  2.0 0.8 copy-done.2
  2.7 0.0 copy-done.5
  2.7 0.0 copy-done.4
  2.7 0.0 copy-start
  2.7 1.2 %copy-done = bf16[8,16,16,192]{3,2,1,0:T(8,128)(2,1)S(1)} copy-done((bf16[8,16,16,192]{3,2,1,0:T(8,128)(2,1)S(1)}, bf16[8,16,16,192]{3,2,1,0:T(8,128)(2,1)}, u32[]{:S(2)}) %copy-start) | copy-done | bytes 786456
  4.0 0.0 copy-start.1
  4.0 1.2 %copy-done.1 = bf16[8,16,16,192]{3,2,1,0:T(8,128)(2,1)S(1)} copy-done((bf16[8,16,16,192]{3,2,1,0:T(8,128)(2,1)S(1)}, bf16[8,16,16,192]{3,2,1,0:T(8,128)(2,1)}, u32[]{:S(2)}) %copy-start.1) | copy-done | bytes 786456
  5.2 73.1 %shard_map.126 = (bf16[8,16,16,192]{3,2,1,0:T(8,128)(2,1)S(1)}, f32[192,576]{1,0:T(8,128)S(1)}, f32[1,576]{1,0:T(1,128)S(1)}, f32[192,192]{1,0:T(8,128)S(1)}, f32[8,192]{1,0:T(8,128)S(1)}) custom-call(bf16[8,16,16,192]{3,2,1,0:T(8,128)(2,1)S(1)} %copy-done, bf16[8,16,16,192]{3,2,1,0:T(8,128)(2,1)S(1)} %copy-done.1, f32[1,192]{1,0:T(1,128)S(1)} %bitcast.7, ...), custom_call_target="tpu_custom_call" | custom-call | tf_op jit(solution)/shard_map/pallas_call | solution.py:349
  78.3 0.6 fusion
  78.8 0.6 reduce
  79.4 1.0 %copy.20 = bf16[8,16,16,192]{3,2,1,0:T(8,128)(2,1)} copy(bf16[8,16,16,192]{3,2,1,0:T(8,128)(2,1)S(1)} %get-tuple-element.27) | data formatting | bytes 1572864
  80.4 0.8 copy.21
  81.2 0.7 copy.22
Async XLA Ops:
  0.6 1.2 %copy-start.6 = (f32[576]{0:T(1024)S(1)}, f32[576]{0:T(1024)}, u32[]{:S(2)}) copy-start(f32[576]{0:T(1024)} %param.12) | copy-start | bytes 6916
  0.6 1.3 %copy-start.3 = (bf16[192,192]{1,0:T(8,128)(2,1)S(1)}, bf16[192,192]{1,0:T(8,128)(2,1)}, u32[]{:S(2)}) copy-start(bf16[192,192]{1,0:T(8,128)(2,1)} %pw_ref.1) | copy-start | bytes 221188
  1.8 0.9 %copy-start.2 = (bf16[192,576]{1,0:T(8,128)(2,1)S(1)}, bf16[192,576]{1,0:T(8,128)(2,1)}, u32[]{:S(2)}) copy-start(bf16[192,576]{1,0:T(8,128)(2,1)} %w_ref.1) | copy-start | bytes 663556
  1.8 0.9 %copy-start.5 = (f32[192]{0:T(256)S(1)}, f32[192]{0:T(256)}, u32[]{:S(2)}) copy-start(f32[192]{0:T(256)} %param.10) | copy-start | bytes 2308
  2.0 0.8 copy-start.4
  2.7 1.2 %copy-start = (bf16[8,16,16,192]{3,2,1,0:T(8,128)(2,1)S(1)}, bf16[8,16,16,192]{3,2,1,0:T(8,128)(2,1)}, u32[]{:S(2)}) copy-start(bf16[8,16,16,192]{3,2,1,0:T(8,128)(2,1)} %tok_ref.1) | copy-start | bytes 2359300
  4.0 1.2 %copy-start.1 = (bf16[8,16,16,192]{3,2,1,0:T(8,128)(2,1)S(1)}, bf16[8,16,16,192]{3,2,1,0:T(8,128)(2,1)}, u32[]{:S(2)}) copy-start(bf16[8,16,16,192]{3,2,1,0:T(8,128)(2,1)} %upw_ref.1) | copy-start | bytes 2359300

commit v2 on v1

--- a/solution.py
+++ b/solution.py
@@ -46,11 +46,11 @@
 
 
 def kernel(
-    counts, width, scale, tok_ref, upw_ref, gain_ref, nbias_ref, wt_ref, w_ref, qbias_ref, pw_ref,
+    counts, width, scale, tok_hbm, upw_hbm, gain_ref, nbias_ref, w_ref, qbias_ref, pw_ref,
     out_ref, qgrad_ref, qbgrad_ref, pgrad_ref, small_ref,
-    cells_ref, wins_ref, res_ref, hid_ref, normed_ref, inv_ref, pk_ref, da_ref, att_ref, pg_ref,
+    tok_ref, upw_ref, wt_ref, cells_ref, wins_ref, res_ref, hid_ref, normed_ref, inv_ref, pk_ref, da_ref, att_ref, pg_ref,
     accq_ref, accp_ref, accs_ref, g_ref, tot_ref, first_ref, got_ref, mine_ref, parts_ref,
-    send_sem, recv_sem, local_sem, pair_send, pair_recv, send2, recv2, send3, recv3,
+    load_sem, send_sem, recv_sem, local_sem, pair_send, pair_recv, send2, recv2, send3, recv3,
 ):
     axes = ("gx", "gy", "gz")
     here = [lax.axis_index(axis) for axis in axes]
@@ -69,6 +69,18 @@
     single = jnp.float32
     half = jnp.bfloat16
 
+    loads = []
+    for a in range(counts[0]):
+        planes = pl.ds(a * SHIFT, SHIFT)
+        for n, (source, target) in enumerate(((tok_hbm, tok_ref), (upw_hbm, upw_ref))):
+            loads.append(
+                pltpu.make_async_copy(
+                    source.at[planes], target.at[planes], load_sem.at[2 * a + n]
+                )
+            )
+    for load in loads:
+        load.start()
+
     barrier = pltpu.get_barrier_semaphore()
     rank = (here[0] * sizes[1] + here[1]) * sizes[2] + here[2]
 
@@ -85,12 +97,15 @@
     lax.fori_loop(1, devices, greet, 0)
 
     order = cell_order(counts[1], counts[2])
-    for x in range(counts[0] * SHIFT):
-        inside = slice(x % SHIFT * area, (x % SHIFT + 1) * area)
-        for source, lanes in ((tok_ref, slice(0, width)), (upw_ref, slice(width, 2 * width))):
-            moved = dot(order, source[x].reshape(plane, width)).astype(half)
-            cells_ref[x // SHIFT, :, inside, lanes] = moved.reshape(-1, area, width)
-    pl.semaphore_wait(barrier, devices - 1)
+
+    def take_in(a):
+        for source, load, start in ((tok_ref, loads[2 * a], 0), (upw_ref, loads[2 * a + 1], width)):
+            load.wait()
+            for x in range(SHIFT):
+                moved = dot(order, source[a * SHIFT + x].reshape(plane, width)).astype(half)
+                cells_ref[a, :, x * area : (x + 1) * area, start : start + width] = moved.reshape(
+                    -1, area, width
+                )
 
     arriving = {}
     for a in range(counts[0]):
@@ -118,9 +133,24 @@
                 else:
                     copy = pltpu.make_async_copy(source, target, local_sem.at[number])
                 arriving[number] = (copy, any(offset))
-    for number in sorted(arriving):
-        arriving[number][0].start()
-
+
+    def send(window, remote):
+        for octant in range(8):
+            copy, far = arriving[window * 8 + octant]
+            if far == remote:
+                copy.start()
+
+    take_in(0)
+    pl.semaphore_wait(barrier, devices - 1)
+    early = counts[0] == 2 and min(counts[1:]) > 2
+    if early:
+        send(0, True)
+    for a in range(1, counts[0]):
+        take_in(a)
+    if not early:
+        send(0, True)
+    send(0, False)
+    wt_ref[...] = w_ref[...].T
     hid_ref[...] = jnp.ones_like(hid_ref)
     accq_ref[...] = jnp.zeros_like(accq_ref)
     accp_ref[...] = jnp.zeros_like(accp_ref)
@@ -139,6 +169,10 @@
                         copy.wait_recv()
                     else:
                         copy.wait()
+                for later in {0: (1, 2)}.get(window, (window + 2,)):
+                    if later < cells // 8:
+                        send(later, True)
+                        send(later, False)
 
         both = wins_ref[step].reshape(length, 2 * width)
         inputs = both[:, :width].astype(single)
@@ -193,7 +227,7 @@
             pg_ref[pl.ds(base + 2 * width, head), :] = vg.astype(half)
             return carry
 
-        lax.fori_loop(0, HEADS, one_head, 0, unroll=1)
+        lax.fori_loop(0, HEADS, one_head, 0, unroll=6)
 
         accq_ref[...] += dot(pg_ref[...], hid_ref[...])
         accp_ref[...] += dot(att_ref[...], up)
@@ -355,9 +389,12 @@
             jax.ShapeDtypeStruct((width, width), single),
             jax.ShapeDtypeStruct((8, width), single),
         ),
-        in_specs=[vmem] * 8,
+        in_specs=[pl.BlockSpec(memory_space=pl.ANY)] * 2 + [vmem] * 5,
         out_specs=(vmem,) * 5,
         scratch_shapes=[
+            pltpu.VMEM(tokens.shape, half),
+            pltpu.VMEM(tokens.shape, half),
+            pltpu.VMEM((3 * width, width), half),
             pltpu.VMEM((counts[0], counts[1] * counts[2], CELL, 2 * width), half),
             pltpu.VMEM((cells // 8, 8, CELL, 2 * width), half),
             pltpu.VMEM((cells // 8, 8, CELL, width), half),
@@ -377,6 +414,7 @@
             pltpu.VMEM((middle, LANES), half),
             pltpu.VMEM((middle, LANES), half),
             pltpu.VMEM((chips, middle // chips, LANES), half),
+            dma((2 * counts[0],)),
             dma((cells,)),
             dma((cells,)),
             dma((cells,)),
@@ -395,7 +433,6 @@
         upstream,
         norm_gain.reshape(1, width),
         norm_bias.reshape(1, width),
-        qkv_weight.T,
         qkv_weight,
         qkv_bias.reshape(3 * width, 1),
         proj_weight,

time: 82.1 us -> 77.2 us (0.940)
  Pallas kernels: 73.1 us -> 67.8 us
    pallas_call x1, Pallas kernels: 73.1 us -> 67.8 us  [per_device(): pl.pallas_call(functools.partial(kernel, counts, width, scale), out_shape...]
    unnamed x18 -> x15, local copies, waits for them, and re-layouts: 6.78 us -> 6.46 us
where the time goes in v2:
time: 77.2 us; the launch traced here: 77 us
  Pallas kernels  67.8 us (88%)
  local copies, waits for them, and re-layouts  7.89 us (10%)
    pallas_call x1, Pallas kernels, per_device(): pl.pallas_call(functools.partial(kernel, counts, width, scale), out_shape...  67.8 us
    unnamed x15, local copies, waits for them, and re-layouts  6.46 us

profile of v2, /device:TPU:0, one launch (start us, length us, event | category | flops | bytes accessed | tf_op | source)
XLA Modules:
  0.0 77.0 jit_solution(5889093625404180751)
XLA Ops:
  0.6 0.0 copy-start.2
  0.6 0.0 copy-start.5
  0.7 0.9 %reshape.26.qbias_ref = f32[576,1]{1,0:T(8,128)S(1)} reshape(f32[576]{0:T(1024)} %param.12) | data formatting | bytes 4608 | tf_op jit(solution)/shard_map/reshape | solution.py:437
  1.5 0.0 copy-start.4
  1.5 0.1 copy-done.2
  1.6 0.0 copy-done.5
  1.6 0.6 copy-done.4
  2.2 0.0 copy-start
  2.2 1.2 %copy-done = bf16[8,16,16,192]{3,2,1,0:T(8,128)(2,1)S(1)} copy-done((bf16[8,16,16,192]{3,2,1,0:T(8,128)(2,1)S(1)}, bf16[8,16,16,192]{3,2,1,0:T(8,128)(2,1)}, u32[]{:S(2)}) %copy-start) | copy-done | bytes 786456
  3.4 0.0 copy-start.1
  3.4 1.2 %copy-done.1 = bf16[8,16,16,192]{3,2,1,0:T(8,128)(2,1)S(1)} copy-done((bf16[8,16,16,192]{3,2,1,0:T(8,128)(2,1)S(1)}, bf16[8,16,16,192]{3,2,1,0:T(8,128)(2,1)}, u32[]{:S(2)}) %copy-start.1) | copy-done | bytes 786456
  4.7 0.0 copy-start.3
  4.7 0.9 %copy-done.3 = bf16[192,192]{1,0:T(8,128)(2,1)S(1)} copy-done((bf16[192,192]{1,0:T(8,128)(2,1)S(1)}, bf16[192,192]{1,0:T(8,128)(2,1)}, u32[]{:S(2)}) %copy-start.3) | copy-done | bytes 73752
  5.6 67.8 %shard_map.126 = (bf16[8,16,16,192]{3,2,1,0:T(8,128)(2,1)S(1)}, f32[192,576]{1,0:T(8,128)S(1)}, f32[1,576]{1,0:T(1,128)S(1)}, f32[192,192]{1,0:T(8,128)S(1)}, f32[8,192]{1,0:T(8,128)S(1)}) custom-call(bf16[8,16,16,192]{3,2,1,0:T(8,128)(2,1)S(1)} %copy-done, bf16[8,16,16,192]{3,2,1,0:T(8,128)(2,1)S(1)} %copy-done.1, f32[1,192]{1,0:T(1,128)S(1)} %bitcast.5, ...), custom_call_target="tpu_custom_call" | custom-call | tf_op jit(solution)/shard_map/pallas_call | solution.py:383
  73.4 0.6 fusion
  73.9 0.6 reduce
  74.5 1.0 %copy.18 = bf16[8,16,16,192]{3,2,1,0:T(8,128)(2,1)} copy(bf16[8,16,16,192]{3,2,1,0:T(8,128)(2,1)S(1)} %get-tuple-element.27) | data formatting | bytes 1572864
  75.5 0.8 %copy.19 = f32[192,576]{1,0:T(8,128)} copy(f32[192,576]{1,0:T(8,128)S(1)} %get-tuple-element.28) | data formatting | bytes 884736
  76.3 0.7 copy.20
Async XLA Ops:
  0.6 1.0 %copy-start.2 = (bf16[192,576]{1,0:T(8,128)(2,1)S(1)}, bf16[192,576]{1,0:T(8,128)(2,1)}, u32[]{:S(2)}) copy-start(bf16[192,576]{1,0:T(8,128)(2,1)} %w_ref.1) | copy-start | bytes 663556
  0.6 1.0 %copy-start.5 = (f32[192]{0:T(256)S(1)}, f32[192]{0:T(256)}, u32[]{:S(2)}) copy-start(f32[192]{0:T(256)} %param.10) | copy-start | bytes 2308
  1.5 0.7 copy-start.4
  2.2 1.2 %copy-start = (bf16[8,16,16,192]{3,2,1,0:T(8,128)(2,1)S(1)}, bf16[8,16,16,192]{3,2,1,0:T(8,128)(2,1)}, u32[]{:S(2)}) copy-start(bf16[8,16,16,192]{3,2,1,0:T(8,128)(2,1)} %tok_hbm.1) | copy-start | bytes 2359300
  3.4 1.2 %copy-start.1 = (bf16[8,16,16,192]{3,2,1,0:T(8,128)(2,1)S(1)}, bf16[8,16,16,192]{3,2,1,0:T(8,128)(2,1)}, u32[]{:S(2)}) copy-start(bf16[8,16,16,192]{3,2,1,0:T(8,128)(2,1)} %upw_hbm.1) | copy-start | bytes 2359300
  4.7 0.9 %copy-start.3 = (bf16[192,192]{1,0:T(8,128)(2,1)S(1)}, bf16[192,192]{1,0:T(8,128)(2,1)}, u32[]{:S(2)}) copy-start(bf16[192,192]{1,0:T(8,128)(2,1)} %pw_ref.1) | copy-start | bytes 221188

commit v3 on v2

--- a/solution.py
+++ b/solution.py
@@ -12,6 +12,7 @@
 SHIFT = 4
 CELL = SHIFT**3
 LANES = 128
+STRIP = 128
 MASKED = -1e30
 MESH = pl.DeviceIdType.MESH
 
@@ -46,10 +47,10 @@
 
 
 def kernel(
-    counts, width, scale, tok_hbm, upw_hbm, gain_ref, nbias_ref, w_ref, qbias_ref, pw_ref,
+    counts, width, scale, tok_hbm, upw_hbm, gain_ref, nbias_ref, w_hbm, qbias_ref, pw_hbm,
     out_ref, qgrad_ref, qbgrad_ref, pgrad_ref, small_ref,
-    tok_ref, upw_ref, wt_ref, cells_ref, wins_ref, res_ref, hid_ref, normed_ref, inv_ref, pk_ref, da_ref, att_ref, pg_ref,
-    accq_ref, accp_ref, accs_ref, g_ref, tot_ref, first_ref, got_ref, mine_ref, parts_ref,
+    tok_ref, upw_ref, w_ref, pw_ref, wt_ref, cells_ref, wins_ref, res_ref, hid_ref, normed_ref, inv_ref, pk_ref, da_ref, att_ref, pg_ref,
+    accq_ref, accp_ref, accs_ref, s_ref, d_ref, ph_ref, ds_ref, qb_ref, g_ref, tot_ref, first_ref, got_ref, mine_ref, parts_ref,
     load_sem, send_sem, recv_sem, local_sem, pair_send, pair_recv, send2, recv2, send3, recv3,
 ):
     axes = ("gx", "gy", "gz")
@@ -78,6 +79,8 @@
                     source.at[planes], target.at[planes], load_sem.at[2 * a + n]
                 )
             )
+    for n, (source, target) in enumerate(((w_hbm, w_ref), (pw_hbm, pw_ref))):
+        loads.append(pltpu.make_async_copy(source, target, load_sem.at[2 * counts[0] + n]))
     for load in loads:
         load.start()
 
@@ -150,6 +153,9 @@
     if not early:
         send(0, True)
     send(0, False)
+    qb_ref[...] = jnp.broadcast_to(qbias_ref[...], (8, 3 * width)).T[:, :1]
+    loads[-2].wait()
+    loads[-1].wait()
     wt_ref[...] = w_ref[...].T
     hid_ref[...] = jnp.ones_like(hid_ref)
     accq_ref[...] = jnp.zeros_like(accq_ref)
@@ -184,7 +190,7 @@
         inv_ref[...] = inverse
         hidden = (normed * gain_ref[...] + nbias_ref[...]).astype(half)
         hid_ref[:, :width] = hidden
-        pk_ref[...] = (dot_nt(wt_ref[...], hidden) + qbias_ref[...]).astype(half)
+        pk_ref[...] = (dot_nt(wt_ref[...], hidden) + qb_ref[...]).astype(half)
         da_ref[...] = dot_nt(pw_ref[...], up).astype(half)
 
         place = (step // (spread[1] * spread[2]), step // spread[2] % spread[1], step % spread[2])
@@ -211,14 +217,30 @@
             vg = jnp.zeros((head, length), single)
             for start in range(0, length, tile):
                 part = slice(start, start + tile)
-                scores = dot(keys, qt_marked[:, part])
-                prob_grad = dot(values, dat[:, part])
-                peak = jnp.max(scores, axis=0, keepdims=True)
-                expo = jnp.exp2((scores - peak) * exponent)
-                probs = expo * (1.0 / jnp.sum(expo, axis=0, keepdims=True))
-                inner = jnp.sum(probs * prob_grad, axis=0, keepdims=True)
-                probs_half = probs.astype(half)
-                score_grad = (probs * (prob_grad - inner)).astype(half)
+                slot = start // tile % 2
+                strips = [slice(at, at + STRIP) for at in range(0, length, STRIP)]
+                peak = jnp.full((1, tile), 2 * MASKED, single)
+                for strip in strips:
+                    scores = dot(keys[strip], qt_marked[:, part])
+                    s_ref[slot, strip, :] = scores
+                    peak = jnp.maximum(peak, jnp.max(scores, axis=0, keepdims=True))
+                norm = jnp.zeros((1, tile), single)
+                inner = jnp.zeros((1, tile), single)
+                for strip in strips:
+                    prob_grad = dot(values[strip], dat[:, part])
+                    expo = jnp.exp2((s_ref[slot, strip, :] - peak) * exponent)
+                    norm += jnp.sum(expo, axis=0, keepdims=True)
+                    inner += jnp.sum(expo * prob_grad, axis=0, keepdims=True)
+                    s_ref[slot, strip, :] = expo
+                    d_ref[slot, strip, :] = prob_grad
+                share = 1.0 / norm
+                inner = inner * share
+                for strip in strips:
+                    probs = s_ref[slot, strip, :] * share
+                    ph_ref[slot, strip, :] = probs.astype(half)
+                    ds_ref[slot, strip, :] = (probs * (d_ref[slot, strip, :] - inner)).astype(half)
+                probs_half = ph_ref[slot]
+                score_grad = ds_ref[slot]
                 att_ref[pl.ds(base, head), part] = dot(vt, probs_half).astype(half)
                 pg_ref[pl.ds(base, head), part] = (dot(kt, score_grad) * factor).astype(half)
                 vg += dot_nt(dat[:, part], probs_half)
@@ -377,6 +399,7 @@
     middle = rows // 2
     scale = float(x * y * z * devices) ** (-0.5)
     vmem = pl.BlockSpec(memory_space=pltpu.VMEM)
+    hbm = pl.BlockSpec(memory_space=pltpu.HBM)
     half = jnp.bfloat16
     single = jnp.float32
     dma = pltpu.SemaphoreType.DMA
@@ -389,11 +412,13 @@
             jax.ShapeDtypeStruct((width, width), single),
             jax.ShapeDtypeStruct((8, width), single),
         ),
-        in_specs=[pl.BlockSpec(memory_space=pl.ANY)] * 2 + [vmem] * 5,
+        in_specs=[hbm, hbm, vmem, vmem, hbm, vmem, hbm],
         out_specs=(vmem,) * 5,
         scratch_shapes=[
             pltpu.VMEM(tokens.shape, half),
             pltpu.VMEM(tokens.shape, half),
+            pltpu.VMEM((width, 3 * width), half),
+            pltpu.VMEM((width, width), half),
             pltpu.VMEM((3 * width, width), half),
             pltpu.VMEM((counts[0], counts[1] * counts[2], CELL, 2 * width), half),
             pltpu.VMEM((cells // 8, 8, CELL, 2 * width), half),
@@ -408,13 +433,18 @@
             pltpu.VMEM((3 * width, 2 * LANES), single),
             pltpu.VMEM((width, width), single),
             pltpu.VMEM((8, width), single),
+            pltpu.VMEM((2, length, min(256, length)), single),
+            pltpu.VMEM((2, length, min(256, length)), single),
+            pltpu.VMEM((2, length, min(256, length)), half),
+            pltpu.VMEM((2, length, min(256, length)), half),
+            pltpu.VMEM((3 * width, 1), single),
             pltpu.VMEM((rows, LANES), single),
             pltpu.VMEM((rows, LANES), half),
             pltpu.VMEM((middle, LANES), half),
             pltpu.VMEM((middle, LANES), half),
             pltpu.VMEM((middle, LANES), half),
             pltpu.VMEM((chips, middle // chips, LANES), half),
-            dma((2 * counts[0],)),
+            dma((2 * counts[0] + 2,)),
             dma((cells,)),
             dma((cells,)),
             dma((cells,)),
@@ -426,7 +456,7 @@
             dma((chips,)),
         ],
         compiler_params=pltpu.CompilerParams(
-            collective_id=0, has_side_effects=True, vmem_limit_bytes=48 * 1024 * 1024
+            collective_id=0, has_side_effects=True, vmem_limit_bytes=63 * 1024 * 1024
         ),
     )(
         tokens,
@@ -434,7 +464,7 @@
         norm_gain.reshape(1, width),
         norm_bias.reshape(1, width),
         qkv_weight,
-        qkv_bias.reshape(3 * width, 1),
+        qkv_bias.reshape(1, 3 * width),
         proj_weight,
     )
     return (token_grad, qgrad, qbgrad[0], pgrad, small[0], small[1], small[2])

time: 77.2 us -> 75.5 us (0.978)
  Pallas kernels: 67.8 us -> 66.5 us
    unnamed x15 -> x9, local copies, waits for them, and re-layouts: 6.46 us -> 4.79 us
    pallas_call x1, Pallas kernels: 67.8 us -> 66.5 us  [per_device(): pl.pallas_call(functools.partial(kernel, counts, width, scale), out_shape...]
    slice x1, local copies, waits for them, and re-layouts: 0.57 us -> 1.38 us  [per_device(): return (token_grad, qgrad, qbgrad[0], pgrad, small[0], small[1], small[2])]
where the time goes in v3:
time: 75.5 us; the launch traced here: 75.1 us
  Pallas kernels  66.5 us (88%)
  local copies, waits for them, and re-layouts  7.44 us (10%)
    pallas_call x1, Pallas kernels, per_device(): pl.pallas_call(functools.partial(kernel, counts, width, scale), out_shape...  66.5 us
    unnamed x9, local copies, waits for them, and re-layouts  4.79 us

profile of v3, /device:TPU:0, one launch (start us, length us, event | category | flops | bytes accessed | tf_op | source)
XLA Modules:
  0.0 75.1 jit_solution(16032142662699557700)
XLA Ops:
  0.6 1.3 %reshape.25.qbias_ref = f32[1,576]{1,0:T(1,128)} reshape(f32[576]{0:T(1024)} %param.12) | data formatting | bytes 4608 | tf_op jit(solution)/shard_map/reshape | solution.py:467
  1.9 66.5 %shard_map.126 = (bf16[8,16,16,192]{3,2,1,0:T(8,128)(2,1)}, f32[192,576]{1,0:T(8,128)}, f32[1,576]{1,0:T(1,128)}, f32[192,192]{1,0:T(8,128)}, f32[8,192]{1,0:T(8,128)}) custom-call(bf16[8,16,16,192]{3,2,1,0:T(8,128)(2,1)} %tok_hbm.1, bf16[8,16,16,192]{3,2,1,0:T(8,128)(2,1)} %upw_hbm.1, f32[1,192]{1,0:T(1,128)} %bitcast.5, f32[1,192]{1,0:T(1,128)} %bitcast.6, ...), custom_call_target="tpu_custom_call" | custom-call | tf_op jit(solution)/shard_map/pallas_call | solution.py:406
  68.4 1.4 %fusion = (f32[1,192]{1,0:T(1,128)}, f32[1,192]{1,0:T(1,128)}, f32[1,192]{1,0:T(1,128)}) fusion(f32[8,192]{1,0:T(8,128)} %get-tuple-element.16), kind=kLoop, calls=%fused_computation | loop fusion | bytes 4608 | tf_op jit(solution)/shard_map/slice | solution.py:470
  69.8 0.0 copy-start.2
  69.8 0.7 copy-done.2
  70.4 0.6 reduce
  71.0 0.0 copy-start
  71.0 2.3 %copy.17 = bf16[8,16,16,192]{3,2,1,0:T(8,128)(2,1)} copy(bf16[8,16,16,192]{3,2,1,0:T(8,128)(2,1)} %get-tuple-element.27) | data formatting | bytes 1572864
  73.4 0.0 copy-done
  73.4 0.0 copy-start.1
  73.4 0.8 %copy.18 = f32[192,576]{1,0:T(8,128)} copy(f32[192,576]{1,0:T(8,128)S(1)} %copy-done) | data formatting | bytes 884736
  74.1 0.3 copy-done.1
  74.5 0.7 copy.19
Async XLA Ops:
  69.8 0.7 copy-start.2
  71.0 2.3 %copy-start = (f32[192,576]{1,0:T(8,128)S(1)}, f32[192,576]{1,0:T(8,128)}, u32[]{:S(2)}) copy-start(f32[192,576]{1,0:T(8,128)} %get-tuple-element.28) | copy-start | bytes 1327108
  73.4 1.1 %copy-start.1 = (f32[192,192]{1,0:T(8,128)S(1)}, f32[192,192]{1,0:T(8,128)}, u32[]{:S(2)}) copy-start(f32[192,192]{1,0:T(8,128)} %get-tuple-element.30) | copy-start | bytes 442372

commit v4 on v3

--- a/solution.py
+++ b/solution.py
@@ -456,7 +456,7 @@
             dma((chips,)),
         ],
         compiler_params=pltpu.CompilerParams(
-            collective_id=0, has_side_effects=True, vmem_limit_bytes=63 * 1024 * 1024
+            collective_id=0, has_side_effects=True, vmem_limit_bytes=48 * 1024 * 1024
         ),
     )(
         tokens,

time: 75.5 us -> 75.8 us (level)
  local copies, waits for them, and re-layouts: 7.44 us -> 8.66 us
  Pallas kernels: 66.5 us -> 65.6 us
    unnamed x9 -> x15, local copies, waits for them, and re-layouts: 4.79 us -> 7.4 us
    pallas_call x1, Pallas kernels: 66.5 us -> 65.6 us  [per_device(): pl.pallas_call(functools.partial(kernel, counts, width, scale), out_shape...]
    slice x1, local copies, waits for them, and re-layouts: 1.38 us -> 0.57 us  [per_device(): return (token_grad, qgrad, qbgrad[0], pgrad, small[0], small[1], small[2])]
where the time goes in v4:
time: 75.8 us; the launch traced here: 75.5 us
  Pallas kernels  65.6 us (87%)
  local copies, waits for them, and re-layouts  8.66 us (11%)
    pallas_call x1, Pallas kernels, per_device(): pl.pallas_call(functools.partial(kernel, counts, width, scale), out_shape...  65.6 us
    unnamed x15, local copies, waits for them, and re-layouts  7.4 us

profile of v4, /device:TPU:0, one launch (start us, length us, event | category | flops | bytes accessed | tf_op | source)
XLA Modules:
  0.0 75.5 jit_solution(17369704438379483626)
XLA Ops:
  0.6 0.7 reshape.25.qbias_ref
  1.3 0.0 copy-start.5
  1.3 0.0 copy-start.4
  1.3 0.7 copy-done.5
  2.0 0.0 copy-done.4
  2.0 0.0 copy-start
  2.0 1.2 %copy-done = bf16[8,16,16,192]{3,2,1,0:T(8,128)(2,1)S(1)} copy-done((bf16[8,16,16,192]{3,2,1,0:T(8,128)(2,1)S(1)}, bf16[8,16,16,192]{3,2,1,0:T(8,128)(2,1)}, u32[]{:S(2)}) %copy-start) | copy-done | bytes 786456
  3.2 0.0 copy-start.1
  3.2 1.2 %copy-done.1 = bf16[8,16,16,192]{3,2,1,0:T(8,128)(2,1)S(1)} copy-done((bf16[8,16,16,192]{3,2,1,0:T(8,128)(2,1)S(1)}, bf16[8,16,16,192]{3,2,1,0:T(8,128)(2,1)}, u32[]{:S(2)}) %copy-start.1) | copy-done | bytes 786456
  4.5 0.0 copy-start.2
  4.5 0.9 %copy-done.2 = bf16[192,576]{1,0:T(8,128)(2,1)S(1)} copy-done((bf16[192,576]{1,0:T(8,128)(2,1)S(1)}, bf16[192,576]{1,0:T(8,128)(2,1)}, u32[]{:S(2)}) %copy-start.2) | copy-done | bytes 221208
  5.4 0.0 copy-start.3
  5.4 0.9 %copy-done.3 = bf16[192,192]{1,0:T(8,128)(2,1)S(1)} copy-done((bf16[192,192]{1,0:T(8,128)(2,1)S(1)}, bf16[192,192]{1,0:T(8,128)(2,1)}, u32[]{:S(2)}) %copy-start.3) | copy-done | bytes 73752
  6.3 65.6 %shard_map.126 = (bf16[8,16,16,192]{3,2,1,0:T(8,128)(2,1)S(1)}, f32[192,576]{1,0:T(8,128)S(1)}, f32[1,576]{1,0:T(1,128)S(1)}, f32[192,192]{1,0:T(8,128)S(1)}, f32[8,192]{1,0:T(8,128)S(1)}) custom-call(bf16[8,16,16,192]{3,2,1,0:T(8,128)(2,1)S(1)} %copy-done, bf16[8,16,16,192]{3,2,1,0:T(8,128)(2,1)S(1)} %copy-done.1, f32[1,192]{1,0:T(1,128)S(1)} %bitcast.5, ...), custom_call_target="tpu_custom_call" | custom-call | tf_op jit(solution)/shard_map/pallas_call | solution.py:406
  71.9 0.6 fusion
  72.5 0.6 reduce
  73.1 1.0 %copy.17 = bf16[8,16,16,192]{3,2,1,0:T(8,128)(2,1)} copy(bf16[8,16,16,192]{3,2,1,0:T(8,128)(2,1)S(1)} %get-tuple-element.27) | data formatting | bytes 1572864
  74.0 0.8 %copy.18 = f32[192,576]{1,0:T(8,128)} copy(f32[192,576]{1,0:T(8,128)S(1)} %get-tuple-element.28) | data formatting | bytes 884736
  74.8 0.7 copy.19
Async XLA Ops:
  1.3 0.7 copy-start.5
  1.3 0.7 copy-start.4
  2.0 1.2 %copy-start = (bf16[8,16,16,192]{3,2,1,0:T(8,128)(2,1)S(1)}, bf16[8,16,16,192]{3,2,1,0:T(8,128)(2,1)}, u32[]{:S(2)}) copy-start(bf16[8,16,16,192]{3,2,1,0:T(8,128)(2,1)} %tok_hbm.1) | copy-start | bytes 2359300
  3.2 1.2 %copy-start.1 = (bf16[8,16,16,192]{3,2,1,0:T(8,128)(2,1)S(1)}, bf16[8,16,16,192]{3,2,1,0:T(8,128)(2,1)}, u32[]{:S(2)}) copy-start(bf16[8,16,16,192]{3,2,1,0:T(8,128)(2,1)} %upw_hbm.1) | copy-start | bytes 2359300
  4.5 0.9 %copy-start.2 = (bf16[192,576]{1,0:T(8,128)(2,1)S(1)}, bf16[192,576]{1,0:T(8,128)(2,1)}, u32[]{:S(2)}) copy-start(bf16[192,576]{1,0:T(8,128)(2,1)} %w_hbm.1) | copy-start | bytes 663556
  5.4 0.9 %copy-start.3 = (bf16[192,192]{1,0:T(8,128)(2,1)S(1)}, bf16[192,192]{1,0:T(8,128)(2,1)}, u32[]{:S(2)}) copy-start(bf16[192,192]{1,0:T(8,128)(2,1)} %pw_hbm.1) | copy-start | bytes 221188
